TPU v7x, 32 devices: a whole 2x2x4 slice. The times are simulated.
32 devices in a mesh: dp: 16 (over z, x, core), seq: 2 (over y).
Axes of the slice: x: 2, y: 2, z: 4, core: 2. Of those that a mesh axis runs over, the one named last changes fastest.
Arguments:
- hidden_in: bfloat16 [16, 260, 1152], P('dp', 'seq'), may hold values from -6 to 6
- skip_in: bfloat16 [16, 260, 1152], P('dp', None, 'seq'), may hold values from -6 to 6
- cotangent: bfloat16 [16, 260, 1152], P('dp', 'seq'), may hold values from -6 to 6
- timesteps: int32 [16], P('dp'), may hold values from 0 to 999, as said below
- counts: int32 [16], P('dp'), may hold values from 1 to 1, as said below
- w_skip: bfloat16 [2304, 1152], replicated, may hold values from -0.125 to 0.125
- w_qkv: bfloat16 [1152, 3456], replicated, may hold values from -0.1875 to 0.1875
- w_proj: bfloat16 [1152, 1152], replicated, may hold values from -0.75 to 0.75
- w_fc1: bfloat16 [1152, 4608], replicated, may hold values from -0.1875 to 0.1875
- w_fc2: bfloat16 [4608, 1152], replicated, may hold values from -0.09375 to 0.09375
- gains: float32 [2, 1152], replicated, may hold values from 0.1 to 1.9
- biases: float32 [5, 1152], replicated, may hold values from -2 to 2
- fc1_bias: float32 [4608], replicated, may hold values from -3 to 3
Outputs:
- output: bfloat16 [16, 260, 1152], P('dp', 'seq')
- grad_hidden: bfloat16 [16, 260, 1152], P('dp', 'seq')
- grad_skip: bfloat16 [16, 260, 1152], P('dp', None, 'seq')
- grad_w_skip: float32 [2304, 1152], P('dp', 'seq')
- grad_w_qkv: float32 [1152, 3456], P('seq', 'dp')
- grad_w_proj: float32 [1152, 1152], P('dp', 'seq')
- grad_w_fc1: float32 [1152, 4608], P('seq', 'dp')
- grad_w_fc2: float32 [4608, 1152], P('dp', 'seq')
- grad_gains: float32 [2, 1152], replicated
- grad_biases: float32 [5, 1152], replicated
- grad_fc1_bias: float32 [4608], replicated
Inputs may be any that keep to these rules, and one draw needn't show every extreme that they name: timesteps; larger ones are more frequent. The first counts[g] of the 1 slots of data group g hold live items, the others are empty; some group is full.
All inputs are finite; a program needn't handle non-finite values.
Results may differ from a plain program's by a relative error of at most 0.015.
Values may be sent and summed in bfloat16 or wider, within the bound.
No kernel may reach another device: no remote copies, remote signals or barrier semaphores. Data moves between devices by JAX's collectives and lax.ppermute only.
A program may use at most 384 MiB of HBM per device.

v0:
```python
from functools import partial

import jax
import jax.numpy as jnp
from jax import lax
from jax.sharding import PartitionSpec as P

HEADS = 16
PADDED = 2
TSTEPS = 1000


EPSILON = 1e-06
NEG_FILL = -1e30


def layer_norm(value, gain, shift):
    center = value - jnp.mean(value, axis=-1, keepdims=True)
    spread = jnp.mean(center * center, axis=-1, keepdims=True)
    return center * lax.rsqrt(spread + EPSILON) * gain + shift


def inner_rows(left, right):
    return lax.dot_general(
        left, right, (((0,), (0,)), ((), ())), preferred_element_type=jnp.float32
    )


def outer_cols(left, right):
    return lax.dot_general(
        left, right, (((1,), (1,)), ((), ())), preferred_element_type=jnp.float32
    )


def shards(
    hidden_in,
    skip_in,
    cotangent,
    timesteps,
    counts,
    w_skip,
    w_qkv,
    w_proj,
    w_fc1,
    w_fc2,
    gains,
    biases,
    fc1_bias,
):
    slot_count, local_len, model_width = hidden_in.shape
    total_len = local_len * lax.axis_size("seq")
    head_dim = model_width // HEADS
    score_scale = head_dim ** (-0.5)
    row_count = slot_count * local_len
    first_pos = lax.axis_index("seq") * local_len
    positions = first_pos + jnp.arange(local_len)
    live_rows = jnp.logical_and(
        jnp.arange(slot_count)[:, None] < counts[0], positions[None, :] < total_len - PADDED
    )
    row_mask = live_rows.astype(jnp.float32).reshape(row_count, 1)
    key_valid = jnp.arange(total_len) < total_len - PADDED
    whole_skip = lax.all_gather(skip_in, "seq", axis=2, tiled=True)
    own_skip = lax.dynamic_slice_in_dim(whole_skip, first_pos, local_len, 1)
    joined = jnp.concatenate([hidden_in, own_skip], axis=-1).reshape(row_count, 2 * model_width)
    merged = jnp.dot(joined, w_skip, preferred_element_type=jnp.float32) + biases[0]
    normed_one = layer_norm(merged, gains[0], biases[1]).astype(jnp.bfloat16)
    project = jnp.dot(normed_one, w_qkv, preferred_element_type=jnp.float32).astype(jnp.bfloat16)
    queries = project[:, :model_width].reshape(slot_count, local_len, HEADS, head_dim)
    keys_local = project[:, model_width : 2 * model_width].reshape(
        slot_count, local_len, model_width
    )
    values_local = project[:, 2 * model_width :].reshape(slot_count, local_len, model_width)
    keys_whole, values_whole = (
        lax.all_gather(keys_local, "seq", axis=1, tiled=True),
        lax.all_gather(values_local, "seq", axis=1, tiled=True),
    )
    keys_heads = keys_whole.reshape(slot_count, total_len, HEADS, head_dim)
    values_heads = values_whole.reshape(slot_count, total_len, HEADS, head_dim)

    def score_block():
        raw = (
            jnp.einsum("sqhd,skhd->shqk", queries, keys_heads, preferred_element_type=jnp.float32)
            * score_scale
        )
        return jnp.where(key_valid, raw, NEG_FILL)

    scores = score_block()
    row_top = jnp.max(scores, axis=-1, keepdims=True)
    log_total = row_top + jnp.log(jnp.sum(jnp.exp(scores - row_top), axis=-1, keepdims=True))
    probs_low = jnp.exp(scores - log_total).astype(jnp.bfloat16)
    mixed = jnp.einsum(
        "shqk,skhd->sqhd", probs_low, values_heads, preferred_element_type=jnp.float32
    )
    mixed = mixed.reshape(row_count, model_width).astype(jnp.bfloat16)
    after_attn = merged + jnp.dot(mixed, w_proj, preferred_element_type=jnp.float32) + biases[2]
    normed_two = layer_norm(after_attn, gains[1], biases[3]).astype(jnp.bfloat16)
    inner = jnp.dot(normed_two, w_fc1, preferred_element_type=jnp.float32) + fc1_bias
    gelu_exact = partial(jax.nn.gelu, approximate=False)
    activ = gelu_exact(inner).astype(jnp.bfloat16)
    result = (
        after_attn + jnp.dot(activ, w_fc2, preferred_element_type=jnp.float32) + biases[4]
    ) * row_mask
    output = result.reshape(slot_count, local_len, model_width).astype(jnp.bfloat16)
    loss_weight = jax.nn.sigmoid(12.0 * timesteps.astype(jnp.float32) / TSTEPS - 6.0)
    grad_out = (cotangent.astype(jnp.float32) * loss_weight[:, None, None]).reshape(
        row_count, model_width
    ) * row_mask
    grad_out_low = grad_out.astype(jnp.bfloat16)
    grad_w_fc2 = inner_rows(activ, grad_out_low)
    grad_activ = outer_cols(grad_out_low, w_fc2)
    unused, gelu_back = jax.vjp(gelu_exact, inner)
    grad_inner = gelu_back(grad_activ)[0]
    grad_inner_low = grad_inner.astype(jnp.bfloat16)
    grad_w_fc1_turned = inner_rows(grad_inner_low, normed_two)
    grad_normed_two = outer_cols(grad_inner_low, w_fc1)
    unused, norm_back_two = jax.vjp(layer_norm, after_attn, gains[1], biases[3])
    grad_norm_in, grad_gain_two, grad_shift_two = norm_back_two(grad_normed_two)
    grad_after = grad_out + grad_norm_in
    grad_after_low = grad_after.astype(jnp.bfloat16)
    grad_w_proj = inner_rows(mixed, grad_after_low)
    grad_mixed = outer_cols(grad_after_low, w_proj).astype(jnp.bfloat16)
    grad_mixed = grad_mixed.reshape(slot_count, local_len, HEADS, head_dim)
    scores = score_block()
    probs = jnp.exp(scores - log_total)
    grad_probs = jnp.einsum(
        "sqhd,skhd->shqk", grad_mixed, values_heads, preferred_element_type=jnp.float32
    )
    grad_scores = probs * (grad_probs - jnp.sum(grad_probs * probs, axis=-1, keepdims=True))
    grad_scores = grad_scores.astype(jnp.bfloat16)
    grad_queries = (
        jnp.einsum("shqk,skhd->sqhd", grad_scores, keys_heads, preferred_element_type=jnp.float32)
        * score_scale
    )
    grad_keys_all = (
        jnp.einsum("shqk,sqhd->skhd", grad_scores, queries, preferred_element_type=jnp.float32)
        * score_scale
    )
    grad_values_all = jnp.einsum(
        "shqk,sqhd->skhd", probs_low, grad_mixed, preferred_element_type=jnp.float32
    )
    grad_keys, grad_values = (
        lax.psum_scatter(
            grad_keys_all.reshape(slot_count, total_len, model_width).astype(jnp.bfloat16),
            "seq",
            scatter_dimension=1,
            tiled=True,
        ).astype(jnp.float32),
        lax.psum_scatter(
            grad_values_all.reshape(slot_count, total_len, model_width).astype(jnp.bfloat16),
            "seq",
            scatter_dimension=1,
            tiled=True,
        ).astype(jnp.float32),
    )
    grad_project = jnp.concatenate(
        [
            grad_queries.reshape(row_count, model_width),
            grad_keys.reshape(row_count, model_width),
            grad_values.reshape(row_count, model_width),
        ],
        axis=-1,
    ).astype(jnp.bfloat16)
    grad_w_qkv_turned = inner_rows(grad_project, normed_one)
    grad_normed_one = outer_cols(grad_project, w_qkv)
    unused, norm_back_one = jax.vjp(layer_norm, merged, gains[0], biases[1])
    grad_norm_first, grad_gain_one, grad_shift_one = norm_back_one(grad_normed_one)
    grad_merged = grad_after + grad_norm_first
    grad_merged_low = grad_merged.astype(jnp.bfloat16)
    grad_w_skip = inner_rows(joined, grad_merged_low)
    grad_joined = outer_cols(grad_merged_low, w_skip)
    grad_hidden = (
        grad_joined[:, :model_width]
        .reshape(slot_count, local_len, model_width)
        .astype(jnp.bfloat16)
    )
    grad_own_skip = grad_joined[:, model_width:].reshape(slot_count, local_len, model_width)
    spread_grad = jnp.zeros((slot_count, total_len, model_width), jnp.float32)
    spread_grad = lax.dynamic_update_slice_in_dim(spread_grad, grad_own_skip, first_pos, 1)
    grad_skip = lax.psum_scatter(
        spread_grad.astype(jnp.bfloat16), "seq", scatter_dimension=2, tiled=True
    )
    groups_dp = lax.axis_size("dp")
    weight_grads = (grad_w_skip, grad_w_qkv_turned, grad_w_proj, grad_w_fc1_turned, grad_w_fc2)
    row_sizes = [piece.shape[0] // groups_dp for piece in weight_grads]
    stacked = jnp.concatenate(
        [
            piece.reshape(groups_dp, size, model_width)
            for piece, size in zip(weight_grads, row_sizes)
        ],
        axis=1,
    )
    summed = lax.psum_scatter(
        stacked.astype(jnp.bfloat16), "seq", scatter_dimension=2, tiled=True
    ).astype(jnp.float32)
    summed = lax.psum_scatter(summed, "dp", scatter_dimension=0, tiled=True)
    summed = summed[0]
    pieces = []
    offset = 0
    for size in row_sizes:
        pieces.append(summed[offset : offset + size])
        offset = offset + size
    out_w_skip = pieces[0]
    out_w_qkv = pieces[1].T
    out_w_proj = pieces[2]
    out_w_fc1 = pieces[3].T
    out_w_fc2 = pieces[4]
    grad_gains_part = jnp.stack([grad_gain_one, grad_gain_two])
    grad_biases_part = jnp.stack(
        [
            jnp.sum(grad_merged, axis=0),
            grad_shift_one,
            jnp.sum(grad_after, axis=0),
            grad_shift_two,
            jnp.sum(grad_out, axis=0),
        ]
    )
    grad_fc1_part = jnp.sum(grad_inner, axis=0)
    grad_gains, grad_biases, grad_fc1_bias = lax.psum(
        (grad_gains_part, grad_biases_part, grad_fc1_part), ("dp", "seq")
    )
    return (
        output,
        grad_hidden,
        grad_skip,
        out_w_skip,
        out_w_qkv,
        out_w_proj,
        out_w_fc1,
        out_w_fc2,
        grad_gains,
        grad_biases,
        grad_fc1_bias,
    )


def solution(mesh):
    return jax.shard_map(
        shards,
        mesh=mesh,
        in_specs=(
            P("dp", "seq", None),
            P("dp", None, "seq"),
            P("dp", "seq", None),
            P("dp"),
            P("dp"),
            P(),
            P(),
            P(),
            P(),
            P(),
            P(),
            P(),
            P(),
        ),
        out_specs=(
            P("dp", "seq", None),
            P("dp", "seq", None),
            P("dp", None, "seq"),
            P("dp", "seq"),
            P("seq", "dp"),
            P("dp", "seq"),
            P("seq", "dp"),
            P("dp", "seq"),
            P(),
            P(),
            P(),
        ),
        check_vma=False,
    )
```

profile of v0, /device:TPU:0, one launch (start us, length us, event | category | flops | bytes accessed | tf_op | source)
XLA Modules:
  0.0 1112.5 jit_solution(14381094380836541070)
XLA Ops:
  11.9 23.4 %all_gather.9 = bf16[1,260,1152]{1,0,2:T(2,128)(2,1)} all-gather(bf16[1,260,576]{1,0,2:T(2,128)(2,1)S(1)} %copy.91), channel_id=1, replica_groups=mesh['dp'=16,'seq'=2] {'seq'}, dimensions={2}, use_global_device_ids=true | all-gather | bytes 898560 | tf_op jit(solution)/shard_map/all_gather | solution.py:62
  35.3 4.0 constant_dynamic-slice_fusion
  46.9 4.8 convolution_convert_fusion.4
  52.6 9.4 all-gather.2
  68.5 11.4 %all-gather.3 = bf16[2,130,1152]{2,1,0:T(8,128)(2,1)} all-gather(bf16[1,130,1152]{2,1,0:T(8,128)(2,1)} %get-tuple-element.66), channel_id=3, replica_groups=mesh['dp'=16,'seq'=2] {'seq'}, dimensions={0}, use_global_device_ids=true | all-gather | bytes 898560 | tf_op jit(solution)/shard_map/all_gather | solution.py:74
  100.7 10.1 fusion.12
  110.8 12.1 %fusion.96 = (f32[4608]{0:T(1024)S(1)}, bf16[130,4608]{1,0:T(8,128)(2,1)S(1)}) fusion(f32[130,4608]{1,0:T(8,128)S(1)} %get-tuple-element.81, bf16[4608,1152]{1,0:T(8,128)(2,1)} %param.22, bf16[1,130,1152]{2,1,0:T(8,128)(2,1)S(1)} %copy-done.16, f32[]{:T(128)} %bitcast.7, f32[130]{0:T(256)S(1)} %and_convert_fusion), kind=kOutput, calls=%fused_computation.171 | convolution fusion | flops 1424512512 | bytes 14529548 | tf_op jit(solution)/shard_map/dot_general | solution.py:30
  146.7 17.6 %fusion.88 = (bf16[144,1152]{1,0:T(8,128)(2,1)}, bf16[144,1152]{1,0:T(8,128)(2,1)}) fusion(bf16[1,260,1152]{2,1,0:T(8,128)(2,1)} %copy.104, bf16[1,260,1152]{2,1,0:T(8,128)(2,1)} %copy.102), kind=kCustom, calls=%all-reduce-scatter.2 | all-reduce-scatter fusion | flops 663553 | bytes 1862144
  172.8 6.1 convolution_convert_fusion
  188.8 4.2 dot_general.98
  194.8 6.1 multiply_reduce_fusion.2
  200.9 5.9 convolution_convert_fusion.1
  208.0 4.5 fusion.3
  212.5 7.1 constant_dynamic-update-slice_fusion.1
  222.4 9.5 constant_dynamic-update-slice_fusion
  231.9 6.2 fusion.2
  238.1 48.1 %copy.108 = bf16[16,1008,1152]{1,0,2:T(8,128)(2,1)} copy(bf16[16,1008,1152]{2,1,0:T(8,128)(2,1)} %fusion.2) | data formatting | bytes 74317824 | tf_op jit(solution)/shard_map/concatenate | solution.py:185
  286.5 4.6 fusion.70
  293.9 4.1 copy.119
  299.1 400.7 %reduce-scatter.12.cloned.1.call-done = bf16[16,1008,576]{1,0,2:T(8,128)(2,1)} async-done(((bf16[16,1008,1152]{1,0,2:T(8,128)(2,1)}), bf16[16,1008,576]{1,0,2:T(8,128)(2,1)}) %reduce-scatter.12.cloned.1.call-update) | async-done | bytes 18579472 | tf_op jit(solution)/shard_map/reduce_scatter | solution.py:192
  699.9 24.8 %copy_convert_fusion = f32[16,1008,576]{1,2,0:T(8,128)} fusion(bf16[16,1008,576]{1,0,2:T(8,128)(2,1)} %reduce-scatter.12.cloned.1.call-done), kind=kLoop, calls=%fused_computation.1 | loop fusion | flops 9289728 | bytes 55738368 | tf_op jit(solution)/shard_map/convert_element_type | solution.py:194
  725.3 10.4 fusion.33
  735.9 41.3 %all-reduce.4 = (f32[2,1152]{1,0:T(2,128)}, f32[5,1152]{1,0:T(8,128)}, f32[4608]{0:T(1024)}) all-reduce(f32[2,1152]{1,0:T(2,128)S(1)} %pad_maximum_fusion.5, f32[5,1152]{1,0:T(8,128)S(1)} %stack.23, f32[4608]{0:T(1024)S(1)} %get-tuple-element.82), channel_id=1, replica_groups=mesh['dp'=16,'seq'=2] {'dp','seq'}, use_global_device_ids=true, to_apply=%region_18.19 | all-reduce | flops 12672 | bytes 101376 | tf_op jit(solution)/shard_map/psum | solution.py:218
  780.7 312.0 %reduce-scatter.14.cloned.1.call-done = f32[1,1008,576]{1,2,0:T(8,128)} async-done(((f32[16,1008,576]{1,2,0:T(8,128)}), f32[1,1008,576]{1,2,0:T(8,128)}) %reduce-scatter.14.cloned.1.call-update) | async-done | bytes 2322448 | tf_op jit(solution)/shard_map/reduce_scatter | solution.py:195
  (160 shorter events, 107.7 us)
Async XLA Ops:
  7.2 90.2 %copy-start = (bf16[1152,1152]{1,0:T(8,128)(2,1)S(1)}, bf16[1152,1152]{1,0:T(8,128)(2,1)}, u32[]{:S(2)}) copy-start(bf16[1152,1152]{1,0:T(8,128)(2,1)} %param.20) | copy-start | bytes 7962628
  7.2 692.7 %reduce-scatter.12.cloned.1.call-start = ((), (), s32[]{:S(2)}) async-start(), calls=%async_computation.3 | async-start | bytes 56623104 | tf_op jit(solution)/shard_map/reduce_scatter | solution.py:192
  35.3 7.6 copy-start.25
  35.3 7.6 copy-start.24
  68.5 20.5 %copy-start.27 = (pred[260]{0:T(512)(128)(4,1)S(1)}, pred[260]{0:T(512)(128)(4,1)}, u32[]{:S(2)}) copy-start(pred[260]{0:T(512)(128)(4,1)} %iota_compare_fusion) | copy-start | bytes 784
  99.0 27.6 %copy-start.4 = (f32[130,1152]{1,0:T(8,128)}, f32[130,1152]{1,0:T(8,128)S(1)}, u32[]{:S(2)}) copy-start(f32[130,1152]{1,0:T(8,128)S(1)} %get-tuple-element.75) | copy-start | bytes 1797124
  100.7 10.1 copy-start.16
  100.7 22.2 %slice-start = ((s8[10616832]{0:T(1024)(128)(4,1)}), s8[4194304]{0:T(1024)(128)(4,1)S(1)}, s32[]{:S(2)}) async-start(s8[10616832]{0:T(1024)(128)(4,1)} %bitcast.203), calls=%async_computation.6 | async-start | bytes 8388608
  100.7 22.2 %slice-start.1 = ((s8[10616832]{0:T(1024)(128)(4,1)}), s8[4194304]{0:T(1024)(128)(4,1)S(1)}, s32[]{:S(2)}) async-start(s8[10616832]{0:T(1024)(128)(4,1)} %bitcast.203), calls=%async_computation.7 | async-start | bytes 8388608
  110.8 12.1 %copy-start.30 = (f32[130,4608]{1,0:T(8,128)}, f32[130,4608]{1,0:T(8,128)S(1)}, u32[]{:S(2)}) copy-start(f32[130,4608]{1,0:T(8,128)S(1)} %get-tuple-element.81) | copy-start | bytes 7188484
  110.8 12.2 %slice-start.2 = ((s8[10616832]{0:T(1024)(128)(4,1)}), s8[2228224]{0:T(1024)(128)(4,1)S(1)}, s32[]{:S(2)}) async-start(s8[10616832]{0:T(1024)(128)(4,1)} %bitcast.203), calls=%async_computation.8 | async-start | bytes 4456448
  144.4 26.5 %copy-start.14 = (bf16[1,130,1152]{2,1,0:T(8,128)(2,1)S(1)}, bf16[1,130,1152]{2,1,0:T(8,128)(2,1)}, u32[]{:S(2)}) copy-start(bf16[1,130,1152]{2,1,0:T(8,128)(2,1)} %copy.122) | copy-start | bytes 898564
  144.4 28.4 %copy-start.5 = (f32[130,1152]{1,0:T(8,128)S(1)}, f32[130,1152]{1,0:T(8,128)}, u32[]{:S(2)}) copy-start(f32[130,1152]{1,0:T(8,128)} %copy-done.4) | copy-start | bytes 1797124
  164.4 8.5 copy-start.10
  165.2 27.8 %collective-permute-start.1 = (bf16[14,1152]{1,0:T(8,128)(2,1)S(1)}, bf16[14,1152]{1,0:T(8,128)(2,1)S(1)}, u32[]{:S(2)}, u32[]{:S(2)}) collective-permute-start(bf16[14,1152]{1,0:T(8,128)(2,1)S(1)} %slice.102), channel_id=1, source_target_pairs={{0,1},{2,3},{4,5},{6,7},{8,9},{10,11},{12,13},{14,15},{16,17},{18,... | collective-permute-start | bytes 96776
  169.2 24.6 %collective-permute-start = (bf16[14,1152]{1,0:T(8,128)(2,1)S(1)}, bf16[14,1152]{1,0:T(8,128)(2,1)S(1)}, u32[]{:S(2)}, u32[]{:S(2)}) collective-permute-start(bf16[14,1152]{1,0:T(8,128)(2,1)S(1)} %slice.101), channel_id=1, source_target_pairs={{0,1},{2,3},{4,5},{6,7},{8,9},{10,11},{12,13},{14,15},{16,17},{18,... | collective-permute-start | bytes 96776
  180.6 6.5 copy-start.15
  183.5 9.5 copy-start.21
  187.0 6.8 copy-start.20
  212.5 7.1 copy-start.18
  222.4 9.5 copy-start.19
  286.2 490.9 %reduce-scatter.16.cloned.1.call-start = ((), (), s32[]{:S(2)}) async-start(), calls=%async_computation.5 | async-start | bytes 1327104
  299.1 793.6 %reduce-scatter.14.cloned.1.call-start = ((), (), s32[]{:S(2)}) async-start(), calls=%async_computation.4 | async-start | bytes 40108032 | tf_op jit(solution)/shard_map/reduce_scatter | solution.py:195
  1099.2 6.6 copy-start.1
  (15 other events, 48.7 us)
Sparse Core Ops, SparseCore 0:
  286.3 413.4 reduce-scatter.11
  702.1 18.4 reduce-scatter.15
  724.9 367.7 reduce-scatter.13
where the time goes:
time: 1120 us; the launch traced here: 1110 us
  waiting for transfers between devices  713 us (64%)
  local copies, waits for them, and re-layouts  144 us (13%)
  blocking collectives  103 us (9%)
  matrix products  97.4 us (9%)
  other arithmetic  33.6 us (3%)
  between operations  16.6 us (1%)
    reduce_scatter x1, waiting for transfers between devices, shards(): lax.psum_scatter(stacked.astype(jnp.bfloat16), 'seq', scatter_dimension=2...  401 us
    reduce_scatter x1, waiting for transfers between devices, shards(): summed = lax.psum_scatter(summed, 'dp', scatter_dimension=0, tiled=True)  312 us
    concatenate x1, local copies, waits for them, and re-layouts, shards(): jnp.concatenate([piece.reshape(groups_dp, size, model_width) for piece, s...  48.1 us
    psum x1, blocking collectives, shards(): lax.psum((grad_gains_part, grad_biases_part, grad_fc1_part), ('dp', 'seq'))  41.3 us
    unnamed x82, local copies, waits for them, and re-layouts  38.4 us
    dot_general x5, matrix products, outer_cols(): lax.dot_general(left, right, (((1,), (1,)), ((), ())), preferred_element_...  28.2 us
    dot_general x5, matrix products, inner_rows(): lax.dot_general(left, right, (((0,), (0,)), ((), ())), preferred_element_...  25.5 us
    convert_element_type x1, other arithmetic, shards(): summed = lax.psum_scatter(stacked.astype(jnp.bfloat16), 'seq', scatter_di...  24.8 us
  transfers between devices with their start and end apart: 5, of which 2 were waited for; matrix products, arithmetic and copies ran while one was open for 7% of the time, Pallas kernels for 0%

commit v1 on v0

v1 whole, which is shorter than its diff:
```python
import jax
import jax.numpy as jnp
from jax import lax
from jax.sharding import PartitionSpec as P

HEADS = 16
PADDED = 2
TSTEPS = 1000

EPSILON = 1e-06
NEG_FILL = -1e30
BF = jnp.bfloat16
F32 = jnp.float32


def dot(left, right, dims):
    return lax.dot_general(left, right, ((dims[:1], dims[1:]), ((), ())), preferred_element_type=F32)


def norm(value):
    center = value - jnp.mean(value, axis=-1, keepdims=True)
    rstd = lax.rsqrt(jnp.mean(center * center, axis=-1, keepdims=True) + EPSILON)
    return center * rstd, rstd


def norm_back(grad, xhat, rstd, gain):
    scaled = grad * gain
    return rstd * (
        scaled
        - jnp.mean(scaled, axis=-1, keepdims=True)
        - xhat * jnp.mean(scaled * xhat, axis=-1, keepdims=True)
    )


def pick(array, index, axis):
    return lax.dynamic_index_in_dim(array, index, axis, keepdims=False)


def shards(
    hidden_in,
    skip_in,
    cotangent,
    timesteps,
    counts,
    w_skip,
    w_qkv,
    w_proj,
    w_fc1,
    w_fc2,
    gains,
    biases,
    fc1_bias,
):
    rows, width = hidden_in.shape[1:]
    half = width // 2
    ff = w_fc1.shape[1]
    head_dim = width // HEADS
    scale = head_dim ** (-0.5)
    n_dp = lax.axis_size("dp")
    bits = n_dp.bit_length() - 1
    pairs = n_dp // 2
    place = lax.axis_index("dp")
    core = place % 2
    seq = lax.axis_index("seq")

    def flat(dp, s):
        return 2 * dp + s

    mirror_perm = [
        (flat(2 * k + c, s), flat(2 * k + s, c)) for k in range(pairs) for c in range(2) for s in range(2)
    ]
    turn = {(0, 0): (1, 0), (1, 0): (1, 1), (1, 1): (0, 1), (0, 1): (0, 0)}
    turn_perm = [
        (flat(2 * k + c, s), flat(2 * k + d[0], d[1])) for k in range(pairs) for (c, s), d in turn.items()
    ]
    turn_back_perm = [(b, a) for a, b in turn_perm]

    def mirror(x):
        return lax.ppermute(x, ("dp", "seq"), mirror_perm)

    def across_seq(x):
        return lax.ppermute(x, "seq", [(0, 1), (1, 0)])

    def across_bit(x, bit):
        return lax.ppermute(x, "dp", [(i, i ^ (1 << bit)) for i in range(n_dp)])

    def across_core(x):
        return across_bit(x, 0)

    def swap_if(flag, a, b, axis):
        return jnp.where(flag, jnp.concatenate([b, a], axis), jnp.concatenate([a, b], axis))

    hidden = mirror(hidden_in[0])
    skip_rows = skip_in[0].reshape(2, rows, half)
    skip_a = mirror(pick(skip_rows, seq, 0))
    skip_b = lax.ppermute(pick(skip_rows, 1 - seq, 0), ("dp", "seq"), turn_perm)
    joined = jnp.concatenate([hidden, swap_if(core == 1, skip_a, skip_b, 1)], axis=1)

    live = (counts[0] > 0).astype(F32)
    home_pos = seq * rows + jnp.arange(rows)[:, None]
    home_mask = jnp.where(home_pos < 2 * rows - PADDED, live, 0.0)
    loss_weight = jax.nn.sigmoid(12.0 * timesteps[0].astype(F32) / TSTEPS - 6.0)
    grad_out_home = cotangent[0].astype(F32) * loss_weight * home_mask
    sum_grad_out = jnp.sum(grad_out_home, axis=0)
    g_home = grad_out_home.astype(BF)
    g_far = across_seq(g_home)
    g_other = across_core(jnp.concatenate([g_home, g_far], 0))
    same = core == seq
    g0, g1, g2, g3 = g_home, g_far, g_other[:rows], g_other[rows:]
    g_all = jnp.where(
        same, jnp.concatenate([g0, g2, g1, g3], 0), jnp.concatenate([g3, g1, g2, g0], 0)
    )
    grad_out = g_all[:rows].astype(F32)

    piece = ff // (4 * pairs)
    quarter = pairs * piece
    w1 = pick(pick(w_fc1.reshape(width, pairs, 2, 2, piece), core, 2), seq, 2).reshape(width, quarter)
    w2 = pick(pick(w_fc2.reshape(pairs, 2, 2, piece, width), core, 1), seq, 1).reshape(quarter, width)
    b1 = pick(pick(fc1_bias.reshape(pairs, 2, 2, piece), core, 1), seq, 1).reshape(quarter)

    merged = dot(joined, w_skip, (1, 0)) + biases[0]
    xhat_one, rstd_one = norm(merged)
    normed_one = (xhat_one * gains[0] + biases[1]).astype(BF)
    project = dot(normed_one, w_qkv, (1, 0)).astype(BF)
    kv_other = across_core(project[:, width:])
    kv = jnp.concatenate([project[:, width:], kv_other], 0)
    queries = project[:, :width].reshape(rows, HEADS, head_dim)
    keys = kv[:, :width].reshape(2 * rows, HEADS, head_dim)
    values = kv[:, width:].reshape(2 * rows, HEADS, head_dim)
    spot = jnp.arange(2 * rows)
    last_half = jnp.where(core == 1, spot < rows, spot >= rows)
    key_valid = jnp.logical_not(jnp.logical_and(last_half, spot % rows >= rows - PADDED))
    scores = jnp.einsum("qhd,khd->hqk", queries, keys, preferred_element_type=F32) * scale
    scores = jnp.where(key_valid, scores, NEG_FILL)
    top = jnp.max(scores, axis=-1, keepdims=True)
    expo = jnp.exp(scores - top)
    probs = expo / jnp.sum(expo, axis=-1, keepdims=True)
    probs_low = probs.astype(BF)
    mixed = jnp.einsum("hqk,khd->qhd", probs_low, values, preferred_element_type=F32)
    mixed = mixed.reshape(rows, width).astype(BF)
    after_attn = merged + dot(mixed, w_proj, (1, 0)) + biases[2]
    xhat_two, rstd_two = norm(after_attn)
    normed_two = (xhat_two * gains[1] + biases[3]).astype(BF)

    n_far = across_seq(normed_two)
    n_other = across_core(normed_two)
    n_other_far = across_core(n_far)
    n_all = jnp.concatenate([normed_two, n_far, n_other, n_other_far], 0)
    inner = dot(n_all, w1, (1, 0)) + b1
    cdf = 0.5 * lax.erfc(-inner * (0.5**0.5))
    activ = (inner * cdf).astype(BF)
    grad_w_fc2 = dot(activ, g_all, (0, 0)).astype(BF)
    grad_activ = dot(g_all, w2, (1, 1))
    grad_inner = grad_activ * (cdf + inner * jnp.exp(-0.5 * inner * inner) * (0.5 / jnp.pi) ** 0.5)
    grad_inner_low = grad_inner.astype(BF)
    grad_w_fc1 = dot(grad_inner_low, n_all, (0, 0)).astype(BF)
    sum_grad_inner = jnp.sum(grad_inner, axis=0)

    def sum_rows(partial):
        low = partial.astype(BF)
        mine = partial[: 2 * rows] + across_core(low[2 * rows :]).astype(F32)
        return mine[:rows] + across_seq(mine[rows:].astype(BF)).astype(F32)

    gn_two = sum_rows(dot(grad_inner_low, w1, (1, 1)))
    mlp_out = sum_rows(dot(activ, w2, (1, 0)))
    result = (after_attn + mlp_out + biases[4]).astype(BF)
    output = mirror(result) * home_mask.astype(BF)

    grad_after = grad_out + norm_back(gn_two, xhat_two, rstd_two, gains[1])
    grad_after_low = grad_after.astype(BF)
    grad_mixed = dot(grad_after_low, w_proj, (1, 1)).astype(BF).reshape(rows, HEADS, head_dim)
    grad_probs = jnp.einsum("qhd,khd->hqk", grad_mixed, values, preferred_element_type=F32)
    grad_scores = probs * (grad_probs - jnp.sum(grad_probs * probs, axis=-1, keepdims=True))
    grad_scores = grad_scores.astype(BF)
    grad_q = jnp.einsum("hqk,khd->qhd", grad_scores, keys, preferred_element_type=F32) * scale
    grad_k = jnp.einsum("hqk,qhd->khd", grad_scores, queries, preferred_element_type=F32) * scale
    grad_v = jnp.einsum("hqk,qhd->khd", probs_low, grad_mixed, preferred_element_type=F32)
    grad_kv = jnp.concatenate([grad_k.reshape(2 * rows, width), grad_v.reshape(2 * rows, width)], 1)
    grad_kv = grad_kv[:rows] + across_core(grad_kv[rows:].astype(BF)).astype(F32)
    grad_project = jnp.concatenate([grad_q.reshape(rows, width), grad_kv], 1).astype(BF)
    gn_one = dot(grad_project, w_qkv, (1, 1))
    grad_merged = grad_after + norm_back(gn_one, xhat_one, rstd_one, gains[0])
    grad_merged_low = grad_merged.astype(BF)
    grad_joined = dot(grad_merged_low, w_skip, (1, 1)).astype(BF)
    grad_hidden = mirror(grad_joined[:, :width])
    grad_skip_halves = grad_joined[:, width:].reshape(rows, 2, half)
    back_a = mirror(pick(grad_skip_halves, core, 1))
    back_b = lax.ppermute(pick(grad_skip_halves, 1 - core, 1), ("dp", "seq"), turn_back_perm)
    grad_skip = swap_if(seq == 1, back_a, back_b, 0)

    def own_half(x):
        return lax.dynamic_slice_in_dim(x, seq * half, half, 1)

    def far_half(x):
        return lax.dynamic_slice_in_dim(x, (1 - seq) * half, half, 1)

    def both(x):
        return jnp.concatenate([x, across_seq(x)], 0)

    def both_half(x):
        return jnp.concatenate([own_half(x), across_seq(far_half(x))], 0)

    grad_w_skip = dot(both(joined), both_half(grad_merged_low), (0, 0)).astype(BF)
    grad_w_qkv = dot(both(grad_project), both_half(normed_one), (0, 0)).astype(BF)
    grad_w_proj = dot(both(mixed), both_half(grad_after_low), (0, 0)).astype(BF)

    def halve(array, bit_list):
        left = list(range(bits - 1, -1, -1))[: array.ndim - 2]
        for bit in bit_list:
            axis = left.index(bit)
            mine = (place >> bit) & 1
            keep = pick(array, mine, axis)
            got = across_bit(pick(array, 1 - mine, axis), bit)
            array = keep.astype(F32) + got.astype(F32)
            left.remove(bit)
            if left:
                array = array.astype(BF)
        return array

    order = list(range(bits))

    def blocks(array, count_bits):
        return array.reshape((2,) * count_bits + (array.shape[0] >> count_bits, array.shape[1]))

    def halve_ff(array):
        left = list(range(bits - 1, 0, -1))
        array = blocks(array, bits - 1)
        for bit in order[1:]:
            axis = left.index(bit)
            mine = (place >> bit) & 1
            keep = pick(array, mine, axis)
            got = across_bit(pick(array, 1 - mine, axis), bit)
            array = keep.astype(F32) + got.astype(F32)
            left.remove(bit)
            if left:
                array = array.astype(BF)
        here = own_half(array)
        there = across_seq(far_half(array).astype(BF)).astype(F32)
        return swap_if(seq == 1, here, there, 0)

    out_w_fc2 = halve_ff(grad_w_fc2)
    out_w_fc1 = halve_ff(grad_w_fc1).T
    out_w_proj = halve(blocks(grad_w_proj, bits), order)
    out_w_qkv = halve(blocks(grad_w_qkv, bits), order).T
    out_w_skip = halve(blocks(grad_w_skip, bits), order)

    fc1_part = jnp.zeros((pairs, 2, 2, piece), F32)
    fc1_part = lax.dynamic_update_slice(
        fc1_part, sum_grad_inner.reshape(pairs, 1, 1, piece), (0, core, seq, 0)
    )
    small = jnp.concatenate(
        [
            jnp.sum(gn_one * xhat_one, axis=0),
            jnp.sum(gn_two * xhat_two, axis=0),
            jnp.sum(grad_merged, axis=0),
            jnp.sum(gn_one, axis=0),
            jnp.sum(grad_after, axis=0),
            jnp.sum(gn_two, axis=0),
            sum_grad_out,
            fc1_part.reshape(ff),
        ]
    ).reshape(-1, 128)
    small = small + across_seq(small)
    for bit in order:
        small = small + across_bit(small, bit)
    small = small.reshape(-1)
    return (
        output[None],
        grad_hidden[None],
        grad_skip[None],
        out_w_skip,
        out_w_qkv,
        out_w_proj,
        out_w_fc1,
        out_w_fc2,
        small[: 2 * width].reshape(2, width),
        small[2 * width : 7 * width].reshape(5, width),
        small[7 * width :],
    )


def solution(mesh):
    return jax.shard_map(
        shards,
        mesh=mesh,
        in_specs=(
            P("dp", "seq", None),
            P("dp", None, "seq"),
            P("dp", "seq", None),
            P("dp"),
            P("dp"),
            P(),
            P(),
            P(),
            P(),
            P(),
            P(),
            P(),
            P(),
        ),
        out_specs=(
            P("dp", "seq", None),
            P("dp", "seq", None),
            P("dp", None, "seq"),
            P("dp", "seq"),
            P("seq", "dp"),
            P("dp", "seq"),
            P("seq", "dp"),
            P("dp", "seq"),
            P(),
            P(),
            P(),
        ),
        check_vma=False,
    )
```

time: 1120 us -> 438 us (0.39)
  waiting for transfers between devices: 713 us -> 151 us
  blocking collectives: 103 us -> 0 us
  starting transfers between devices: 5.23 us -> 67.5 us
  local copies, waits for them, and re-layouts: 144 us -> 95.1 us
  matrix products: 97.4 us -> 70.4 us
  between operations: 16.6 us -> 3.53 us
    reduce_scatter x2 -> x0, waiting for transfers between devices: 713 us -> none  [the longest x1 401 us: shards(): lax.psum_scatter(stacked.astype(jnp.bfloat16), 'seq', scatter_dimension=2...]
    ppermute x0 -> x49, waiting for transfers between devices: none -> 151 us  [the longest x29 119 us: across_bit(): return lax.ppermute(x, 'dp', [(i, i ^ 1 << bit) for i in range(n_dp)])]
    ppermute x0 -> x49, starting transfers between devices: none -> 67.5 us  [the longest x29 36.8 us: across_bit(): return lax.ppermute(x, 'dp', [(i, i ^ 1 << bit) for i in range(n_dp)])]
    concatenate x1, local copies, waits for them, and re-layouts: 48.1 us -> 0.01 us  [shards(): jnp.concatenate([jnp.sum(gn_one * xhat_one, axis=0), jnp.sum(gn_two * xha...]
    all_gather x3 -> x0, blocking collectives: 44.1 us -> none  [the longest x1 23.4 us: shards(): whole_skip = lax.all_gather(skip_in, 'seq', axis=2, tiled=True)]
    psum x1 -> x0, blocking collectives: 41.3 us -> none  [shards(): lax.psum((grad_gains_part, grad_biases_part, grad_fc1_part), ('dp', 'seq'))]
    dot_general x21, matrix products: 97.4 us -> 70.4 us  [the longest x15 59.4 us: dot(): lax.dot_general(left, right, ((dims[:1], dims[1:]), ((), ())), preferred_...]
    unnamed x1 -> x0, blocking collectives: 17.6 us -> none
  transfers between devices with their start and end apart: 5 -> 49, of which waited for: 2 -> 16; matrix products, arithmetic and copies ran while one was open for 7% -> 47% of each run, Pallas kernels for 0% -> 0%
where the time goes in v1:
time: 438 us; the launch traced here: 431 us
  waiting for transfers between devices  151 us (34%)
  local copies, waits for them, and re-layouts  95.1 us (22%)
  matrix products  70.4 us (16%)
  starting transfers between devices  67.5 us (15%)
  other arithmetic  44.2 us (10%)
    ppermute x29, waiting for transfers between devices, across_bit(): return lax.ppermute(x, 'dp', [(i, i ^ 1 << bit) for i in range(n_dp)])  119 us
    dot_general x15, matrix products, dot(): lax.dot_general(left, right, ((dims[:1], dims[1:]), ((), ())), preferred_...  59.4 us
    ppermute x29, starting transfers between devices, across_bit(): return lax.ppermute(x, 'dp', [(i, i ^ 1 << bit) for i in range(n_dp)])  36.8 us
    ppermute x13, waiting for transfers between devices, across_seq(): return lax.ppermute(x, 'seq', [(0, 1), (1, 0)])  31.5 us
    unnamed x129, local copies, waits for them, and re-layouts  22.3 us
    ppermute x13, starting transfers between devices, across_seq(): return lax.ppermute(x, 'seq', [(0, 1), (1, 0)])  14.6 us
    ppermute x5, starting transfers between devices, mirror(): return lax.ppermute(x, ('dp', 'seq'), mirror_perm)  12.5 us
    dynamic_slice x7, local copies, waits for them, and re-layouts, pick(): return lax.dynamic_index_in_dim(array, index, axis, keepdims=False)  12.1 us
  transfers between devices with their start and end apart: 49, of which 16 were waited for; matrix products, arithmetic and copies ran while one was open for 47% of the time, Pallas kernels for 0%

profile of v1, /device:TPU:0, one launch (start us, length us, event | category | flops | bytes accessed | tf_op | source)
XLA Modules:
  0.0 431.2 jit_solution(6462975709442554098)
XLA Ops:
  17.5 15.2 %copy.67 = bf16[1152,4608]{0,1:T(8,128)(2,1)} copy(bf16[1152,4608]{1,0:T(8,128)(2,1)} %param.21) | data formatting | bytes 21233664 | tf_op args[8]
  32.7 3.6 constant_dynamic-slice_fusion.16
  43.2 3.7 fusion.103
  47.3 4.8 %convolution_convert_fusion.3 = bf16[130,3456]{1,0:T(8,128)(2,1)S(1)} fusion(bf16[130,1152]{1,0:T(8,128)(2,1)S(1)} %add_convert_fusion.1, bf16[1152,3456]{1,0:T(8,128)(2,1)} %param.19), kind=kOutput, calls=%fused_computation.4 | convolution fusion | flops 1035590400 | bytes 9160704 | tf_op jit(solution)/shard_map/dot_general | solution.py:17
  84.4 7.0 %collective-permute-done.4 = bf16[130,1152]{1,0:T(8,128)(2,1)S(1)} collective-permute-done((bf16[130,1152]{1,0:T(8,128)(2,1)S(1)}, bf16[130,1152]{1,0:T(8,128)(2,1)S(1)}, u32[]{:S(2)}, u32[]{:S(2)}) %collective-permute-start.4) | collective-permute-done | bytes 299552 | tf_op jit(solution)/shard_map/ppermute | solution.py:82
  93.3 15.2 %multiply_convert_fusion.1 = (bf16[520,1152]{1,0:T(8,128)(2,1)S(1)}, f32[520,1152]{1,0:T(8,128)S(1)}, f32[520,1152]{1,0:T(8,128)S(1)}) fusion(f32[1152]{0:T(1024)S(1)} %copy-done.53, bf16[1152,1152]{0,1:T(8,128)(2,1)S(1)} %bitcast.191, bf16[130,1152]{1,0:T(8,128)(2,1)S(1)} %collective-permute-done.6, bf16[130,1152]{1,0:T(8,128)(2,1)S(1)} %collective-permute-done.5, ...), kind=kOutput, calls=%fused_computation.37 | convolution fusion | flops 1424517120 | bytes 9847296 | tf_op jit(solution)/shard_map/dot_general | solution.py:17
  135.7 6.6 %collective-permute-done.13 = bf16[130,1152]{1,0:T(8,128)(2,1)S(1)} collective-permute-done((bf16[130,1152]{1,0:T(8,128)(2,1)S(1)}, bf16[130,1152]{1,0:T(8,128)(2,1)S(1)}, u32[]{:S(2)}, u32[]{:S(2)}) %collective-permute-start.13) | collective-permute-done | bytes 299552 | tf_op jit(solution)/shard_map/ppermute | solution.py:82
  142.7 5.8 %collective-permute-done.8 = bf16[130,1152]{1,0:T(8,128)(2,1)S(1)} collective-permute-done((bf16[130,1152]{1,0:T(8,128)(2,1)S(1)}, bf16[130,1152]{1,0:T(8,128)(2,1)S(1)}, u32[]{:S(2)}, u32[]{:S(2)}) %collective-permute-start.8) | collective-permute-done | bytes 299552 | tf_op jit(solution)/shard_map/ppermute | solution.py:82
  162.4 3.8 collective-permute-start.9
  192.7 19.8 %collective-permute-done.40 = bf16[2,2,144,1152]{3,2,0,1:T(8,128)(2,1)} collective-permute-done((bf16[2,2,144,1152]{3,2,0,1:T(8,128)(2,1)}, bf16[2,2,144,1152]{3,2,0,1:T(8,128)(2,1)}, u32[]{:S(2)}, u32[]{:S(2)}) %collective-permute-start.40) | collective-permute-done | bytes 1327136 | tf_op jit(solution)/shard_map/ppermute | solution.py:85
  216.5 6.5 %multiply_reduce_fusion.2 = (f32[1152]{0:T(1024)S(1)}, f32[130]{0:T(256)S(1)}, f32[130]{0:T(256)S(1)}, f32[1152]{0:T(1024)S(1)}, f32[130,1152]{1,0:T(8,128)S(1)}) fusion(f32[130,1152]{1,0:T(8,128)S(1)} %get-tuple-element.56, f32[130]{0:T(256)S(1)} %copy-done.52, f32[130]{0:T(256)S(1)} %copy-done.46, f32[1152]{0:T(1024)S(1)} %copy-done.41, ...), kind=kOutput, calls=%fused_computation.131 | convolution fusion | flops 1038283520 | bytes 10075168 | tf_op jit(solution)/shard_map/dot_general | solution.py:17
  238.0 6.8 %collective-permute-done.19 = bf16[130,576]{1,0:T(8,128)(2,1)S(1)} collective-permute-done((bf16[130,576]{1,0:T(8,128)(2,1)S(1)}, bf16[130,576]{1,0:T(8,128)(2,1)S(1)}, u32[]{:S(2)}, u32[]{:S(2)}) %collective-permute-start.19) | collective-permute-done | bytes 149792 | tf_op jit(solution)/shard_map/ppermute | solution.py:82
  245.3 4.2 convolution_convert_fusion.4
  249.5 4.5 %copy.78 = bf16[2304,576]{1,0:T(8,128)(2,1)} copy(bf16[2304,576]{0,1:T(8,128)(2,1)} %convolution_convert_fusion.4) | data formatting | bytes 5308416 | tf_op jit(solution)/shard_map/convert_element_type | solution.py:203
  261.3 26.7 %collective-permute-done.47 = f32[99,128]{1,0:T(8,128)S(1)} collective-permute-done((f32[99,128]{1,0:T(8,128)S(1)}, f32[99,128]{1,0:T(8,128)S(1)}, u32[]{:S(2)}, u32[]{:S(2)}) %collective-permute-start.47) | collective-permute-done | bytes 50720 | tf_op jit(solution)/shard_map/ppermute | solution.py:85
  288.0 3.8 collective-permute-start.15
  303.3 6.9 %collective-permute-done.33 = bf16[2,2,72,576]{3,2,1,0:T(8,128)(2,1)S(1)} collective-permute-done((bf16[2,2,72,576]{3,2,1,0:T(8,128)(2,1)S(1)}, bf16[2,2,72,576]{3,2,1,0:T(8,128)(2,1)S(1)}, u32[]{:S(2)}, u32[]{:S(2)}) %collective-permute-start.33) | collective-permute-done | bytes 331808 | tf_op jit(solution)/shard_map/ppermute | solution.py:85
  318.6 5.5 %convolution_convert_fusion.2 = bf16[3456,576]{0,1:T(8,128)(2,1)} fusion(bf16[130,3456]{1,0:T(8,128)(2,1)} %collective-permute-done.24, bf16[130,2304]{1,0:T(8,128)(2,1)S(1)} %copy-done.28, bf16[130,1152]{1,0:T(8,128)(2,1)S(1)} %copy-done.34, bf16[130,576]{1,0:T(8,128)(2,1)} %collective-permute-done.25, bf16[130,576]{1,0:T(8,128)(2,1)S(1)} %get-tuple-element.51), kind=kOutput, calls=%fused_computation.3 | convolution fusion | flops 1043122176 | bytes 6077952 | tf_op jit(solution)/shard_map/dot_general | solution.py:17
  324.1 6.5 %copy.79 = bf16[3456,576]{1,0:T(8,128)(2,1)} copy(bf16[3456,576]{0,1:T(8,128)(2,1)} %convolution_convert_fusion.2) | data formatting | bytes 7962624 | tf_op jit(solution)/shard_map/convert_element_type | solution.py:204
  345.4 12.3 %collective-permute-start.21 = (bf16[2,2,144,576]{3,2,1,0:T(8,128)(2,1)S(1)}, bf16[2,2,144,576]{3,2,1,0:T(8,128)(2,1)S(1)}, u32[]{:S(2)}, u32[]{:S(2)}) collective-permute-start(bf16[2,2,144,576]{3,2,1,0:T(8,128)(2,1)S(1)} %dynamic-slice_bitcast_fusion.4), channel_id=1, source_target_pairs={{0,4},{2,6},{4,0},{6,2},{8,12},{10,14},{12,8},{14,10},{16,20},{18,... | collective-permute-start | bytes 1990664 | tf_op jit(solution)/shard_map/ppermute | solution.py:85
  359.1 15.9 %collective-permute-done.21 = bf16[2,2,144,576]{3,2,1,0:T(8,128)(2,1)S(1)} collective-permute-done((bf16[2,2,144,576]{3,2,1,0:T(8,128)(2,1)S(1)}, bf16[2,2,144,576]{3,2,1,0:T(8,128)(2,1)S(1)}, u32[]{:S(2)}, u32[]{:S(2)}) %collective-permute-start.21) | collective-permute-done | bytes 663584 | tf_op jit(solution)/shard_map/ppermute | solution.py:85
  375.4 22.0 %collective-permute-done.27 = bf16[2,2,216,576]{3,2,1,0:T(8,128)(2,1)S(1)} collective-permute-done((bf16[2,2,216,576]{3,2,1,0:T(8,128)(2,1)S(1)}, bf16[2,2,216,576]{3,2,1,0:T(8,128)(2,1)S(1)}, u32[]{:S(2)}, u32[]{:S(2)}) %collective-permute-start.27) | collective-permute-done | bytes 995360 | tf_op jit(solution)/shard_map/ppermute | solution.py:85
  402.3 12.7 %collective-permute-done.28 = bf16[2,216,576]{2,1,0:T(8,128)(2,1)S(1)} collective-permute-done((bf16[2,216,576]{2,1,0:T(8,128)(2,1)S(1)}, bf16[2,216,576]{2,1,0:T(8,128)(2,1)S(1)}, u32[]{:S(2)}, u32[]{:S(2)}) %collective-permute-start.28) | collective-permute-done | bytes 497696 | tf_op jit(solution)/shard_map/ppermute | solution.py:85
  417.6 10.8 %collective-permute-done.29 = bf16[216,576]{1,0:T(8,128)(2,1)S(1)} collective-permute-done((bf16[216,576]{1,0:T(8,128)(2,1)S(1)}, bf16[216,576]{1,0:T(8,128)(2,1)S(1)}, u32[]{:S(2)}, u32[]{:S(2)}) %collective-permute-start.29) | collective-permute-done | bytes 248864 | tf_op jit(solution)/shard_map/ppermute | solution.py:85
  (355 shorter events, 196.9 us)
Async XLA Ops:
  2.6 38.6 %collective-permute-start.2 = (bf16[130,576]{1,0:T(8,128)(2,1)}, bf16[130,576]{1,0:T(8,128)(2,1)S(1)}, u32[]{:S(2)}, u32[]{:S(2)}) collective-permute-start(bf16[130,576]{1,0:T(8,128)(2,1)} %get-tuple-element.44), channel_id=1, source_target_pairs={{0,0},{1,2},{2,1},{3,3},{4,4},{5,6},{6,5},{7,7},{8,8},{9,10},{10,9... | collective-permute-start | bytes 449288 | tf_op jit(solution)/shard_map/ppermute | solution.py:79
  4.2 37.0 %collective-permute-start.1 = (bf16[130,576]{1,0:T(8,128)(2,1)S(1)}, bf16[130,576]{1,0:T(8,128)(2,1)}, u32[]{:S(2)}, u32[]{:S(2)}) collective-permute-start(bf16[130,576]{1,0:T(8,128)(2,1)S(1)} %get-tuple-element.43), channel_id=1, source_target_pairs={{0,2},{2,3},{3,1},{1,0},{4,6},{6,7},{7,5},{5,4},{8,10},{10,11},{11... | collective-permute-start | bytes 449288 | tf_op jit(solution)/shard_map/ppermute | solution.py:96
  7.6 34.8 %collective-permute-start = (bf16[130,1152]{1,0:T(8,128)(2,1)}, bf16[130,1152]{1,0:T(8,128)(2,1)S(1)}, u32[]{:S(2)}, u32[]{:S(2)}) collective-permute-start(bf16[130,1152]{1,0:T(8,128)(2,1)} %bitcast.205), channel_id=1, source_target_pairs={{0,0},{1,2},{2,1},{3,3},{4,4},{5,6},{6,5},{7,7},{8,8},{9,10},{10,9... | collective-permute-start | bytes 898568 | tf_op jit(solution)/shard_map/ppermute | solution.py:79
  13.0 40.0 %collective-permute-start.10 = (bf16[130,1152]{1,0:T(8,128)(2,1)}, bf16[130,1152]{1,0:T(8,128)(2,1)}, u32[]{:S(2)}, u32[]{:S(2)}) collective-permute-start(bf16[130,1152]{1,0:T(8,128)(2,1)} %get-tuple-element.48), channel_id=1, source_target_pairs={{0,1},{1,0},{2,3},{3,2},{4,5},{5,4},{6,7},{7,6},{8,9},{9,8},{10,11... | collective-permute-start | bytes 898568 | tf_op jit(solution)/shard_map/ppermute | solution.py:82
  58.4 24.9 %collective-permute-start.11 = (bf16[260,1152]{1,0:T(8,128)(2,1)}, bf16[260,1152]{1,0:T(8,128)(2,1)}, u32[]{:S(2)}, u32[]{:S(2)}) collective-permute-start(bf16[260,1152]{1,0:T(8,128)(2,1)} %pad_maximum_fusion.5), channel_id=1, source_target_pairs={{0,2},{2,0},{4,6},{6,4},{8,10},{10,8},{12,14},{14,12},{16,18},{18,... | collective-permute-start | bytes 1797128 | tf_op jit(solution)/shard_map/ppermute | solution.py:85
  60.9 177.1 %collective-permute-start.18 = (bf16[130,2304]{1,0:T(8,128)(2,1)}, bf16[130,2304]{1,0:T(8,128)(2,1)}, u32[]{:S(2)}, u32[]{:S(2)}) collective-permute-start(bf16[130,2304]{1,0:T(8,128)(2,1)} %pad_maximum_fusion.3), channel_id=1, source_target_pairs={{0,1},{1,0},{2,3},{3,2},{4,5},{5,4},{6,7},{7,6},{8,9},{9,8},{10,11... | collective-permute-start | bytes 1797128 | tf_op jit(solution)/shard_map/ppermute | solution.py:82
  83.1 96.6 %collective-permute-start.30 = (bf16[130,1152]{1,0:T(8,128)(2,1)}, bf16[130,1152]{1,0:T(8,128)(2,1)}, u32[]{:S(2)}, u32[]{:S(2)}) collective-permute-start(bf16[130,1152]{1,0:T(8,128)(2,1)} %convert_element_type.331), channel_id=1, source_target_pairs={{0,1},{1,0},{2,3},{3,2},{4,5},{5,4},{6,7},{7,6},{8,9},{9,8},{10,11... | collective-permute-start | bytes 898568 | tf_op jit(solution)/shard_map/ppermute | solution.py:82
  125.3 65.5 %collective-permute-start.36 = (bf16[2,2,144,1152]{3,2,0,1:T(8,128)(2,1)}, bf16[2,2,144,1152]{3,2,0,1:T(8,128)(2,1)}, u32[]{:S(2)}, u32[]{:S(2)}) collective-permute-start(bf16[2,2,144,1152]{3,2,0,1:T(8,128)(2,1)} %bitcast.174), channel_id=1, source_target_pairs={{0,4},{2,6},{4,0},{6,2},{8,12},{10,14},{12,8},{14,10},{16,20},{18,... | collective-permute-start | bytes 3981320 | tf_op jit(solution)/shard_map/ppermute | solution.py:85
  162.4 26.4 %collective-permute-start.9 = (bf16[130,1152]{1,0:T(8,128)(2,1)}, bf16[130,1152]{1,0:T(8,128)(2,1)}, u32[]{:S(2)}, u32[]{:S(2)}) collective-permute-start(bf16[130,1152]{1,0:T(8,128)(2,1)} %get-tuple-element.40), channel_id=1, source_target_pairs={{0,0},{1,2},{2,1},{3,3},{4,4},{5,6},{6,5},{7,7},{8,8},{9,10},{10,9... | collective-permute-start | bytes 898568 | tf_op jit(solution)/shard_map/ppermute | solution.py:79
  179.7 133.0 %collective-permute-start.25 = (bf16[130,576]{1,0:T(8,128)(2,1)}, bf16[130,576]{1,0:T(8,128)(2,1)}, u32[]{:S(2)}, u32[]{:S(2)}) collective-permute-start(bf16[130,576]{1,0:T(8,128)(2,1)} %get-tuple-element.52), channel_id=1, source_target_pairs={{0,1},{1,0},{2,3},{3,2},{4,5},{5,4},{6,7},{7,6},{8,9},{9,8},{10,11... | collective-permute-start | bytes 449288 | tf_op jit(solution)/shard_map/ppermute | solution.py:82
  182.0 30.5 %collective-permute-start.40 = (bf16[2,2,144,1152]{3,2,0,1:T(8,128)(2,1)}, bf16[2,2,144,1152]{3,2,0,1:T(8,128)(2,1)}, u32[]{:S(2)}, u32[]{:S(2)}) collective-permute-start(bf16[2,2,144,1152]{3,2,0,1:T(8,128)(2,1)} %bitcast.198), channel_id=1, source_target_pairs={{0,4},{2,6},{4,0},{6,2},{8,12},{10,14},{12,8},{14,10},{16,20},{18,... | collective-permute-start | bytes 3981320 | tf_op jit(solution)/shard_map/ppermute | solution.py:85
  188.8 27.5 %collective-permute-start.14 = (bf16[130,2304]{1,0:T(8,128)(2,1)}, bf16[130,2304]{1,0:T(8,128)(2,1)S(1)}, u32[]{:S(2)}, u32[]{:S(2)}) collective-permute-start(bf16[130,2304]{1,0:T(8,128)(2,1)} %fusion.36), channel_id=1, source_target_pairs={{0,2},{2,0},{4,6},{6,4},{8,10},{10,8},{12,14},{14,12},{16,18},{18,... | collective-permute-start | bytes 1797128 | tf_op jit(solution)/shard_map/ppermute | solution.py:85
  190.8 101.0 %collective-permute-start.32 = (bf16[2,2,2,72,576]{4,3,2,1,0:T(8,128)(2,1)}, bf16[2,2,2,72,576]{4,3,2,1,0:T(8,128)(2,1)}, u32[]{:S(2)}, u32[]{:S(2)}) collective-permute-start(bf16[2,2,2,72,576]{4,3,2,1,0:T(8,128)(2,1)} %dynamic-slice_bitcast_fusion.3), channel_id=1, source_target_pairs={{0,2},{2,0},{4,6},{6,4},{8,10},{10,8},{12,14},{14,12},{16,18},{18,... | collective-permute-start | bytes 1990664 | tf_op jit(solution)/shard_map/ppermute | solution.py:85
  233.0 25.3 %collective-permute-start.17 = (bf16[130,576]{1,0:T(8,128)(2,1)}, bf16[130,576]{1,0:T(8,128)(2,1)S(1)}, u32[]{:S(2)}, u32[]{:S(2)}) collective-permute-start(bf16[130,576]{1,0:T(8,128)(2,1)} %bitcast.175), channel_id=1, source_target_pairs={{0,0},{1,2},{2,1},{3,3},{4,4},{5,6},{6,5},{7,7},{8,8},{9,10},{10,9... | collective-permute-start | bytes 449288 | tf_op jit(solution)/shard_map/ppermute | solution.py:79
  256.8 42.4 %collective-permute-start.37 = (bf16[2,144,1152]{2,1,0:T(8,128)(2,1)S(1)}, bf16[2,144,1152]{2,1,0:T(8,128)(2,1)}, u32[]{:S(2)}, u32[]{:S(2)}) collective-permute-start(bf16[2,144,1152]{2,1,0:T(8,128)(2,1)S(1)} %copy-done.38), channel_id=1, source_target_pairs={{0,8},{2,10},{4,12},{6,14},{8,0},{10,2},{12,4},{14,6},{16,24},{18,... | collective-permute-start | bytes 1990664 | tf_op jit(solution)/shard_map/ppermute | solution.py:85
  258.3 74.3 %collective-permute-start.41 = (bf16[2,144,1152]{2,1,0:T(8,128)(2,1)}, bf16[2,144,1152]{2,1,0:T(8,128)(2,1)}, u32[]{:S(2)}, u32[]{:S(2)}) collective-permute-start(bf16[2,144,1152]{2,1,0:T(8,128)(2,1)} %dynamic-slice_bitcast_fusion.5), channel_id=1, source_target_pairs={{0,8},{2,10},{4,12},{6,14},{8,0},{10,2},{12,4},{14,6},{16,24},{18,... | collective-permute-start | bytes 1990664 | tf_op jit(solution)/shard_map/ppermute | solution.py:85
  258.9 29.1 %collective-permute-start.47 = (f32[99,128]{1,0:T(8,128)S(1)}, f32[99,128]{1,0:T(8,128)S(1)}, u32[]{:S(2)}, u32[]{:S(2)}) collective-permute-start(f32[99,128]{1,0:T(8,128)S(1)} %add.402), channel_id=1, source_target_pairs={{0,8},{2,10},{4,12},{6,14},{8,0},{10,2},{12,4},{14,6},{16,24},{18,... | collective-permute-start | bytes 152072 | tf_op jit(solution)/shard_map/ppermute | solution.py:85
  299.2 44.4 %collective-permute-start.20 = (bf16[2,2,2,144,576]{4,3,2,1,0:T(8,128)(2,1)}, bf16[2,2,2,144,576]{4,3,2,1,0:T(8,128)(2,1)}, u32[]{:S(2)}, u32[]{:S(2)}) collective-permute-start(bf16[2,2,2,144,576]{4,3,2,1,0:T(8,128)(2,1)} %dynamic-slice_bitcast_fusion.1), channel_id=1, source_target_pairs={{0,2},{2,0},{4,6},{6,4},{8,10},{10,8},{12,14},{14,12},{16,18},{18,... | collective-permute-start | bytes 3981320 | tf_op jit(solution)/shard_map/ppermute | solution.py:85
  310.2 30.6 %collective-permute-start.38 = (bf16[144,1152]{1,0:T(8,128)(2,1)}, bf16[144,1152]{1,0:T(8,128)(2,1)}, u32[]{:S(2)}, u32[]{:S(2)}) collective-permute-start(bf16[144,1152]{1,0:T(8,128)(2,1)} %dynamic-slice_bitcast_fusion.11), channel_id=1, source_target_pairs={{0,16},{2,18},{4,20},{6,22},{8,24},{10,26},{12,28},{14,30},{16,0},... | collective-permute-start | bytes 995336 | tf_op jit(solution)/shard_map/ppermute | solution.py:85
  332.5 25.2 %collective-permute-start.26 = (bf16[2,2,2,216,576]{4,3,2,1,0:T(8,128)(2,1)S(1)}, bf16[2,2,2,216,576]{4,3,2,1,0:T(8,128)(2,1)S(1)}, u32[]{:S(2)}, u32[]{:S(2)}) collective-permute-start(bf16[2,2,2,216,576]{4,3,2,1,0:T(8,128)(2,1)S(1)} %dynamic-slice_bitcast_fusion), channel_id=1, source_target_pairs={{0,2},{2,0},{4,6},{6,4},{8,10},{10,8},{12,14},{14,12},{16,18},{18,... | collective-permute-start | bytes 5971976 | tf_op jit(solution)/shard_map/ppermute | solution.py:85
  342.1 56.0 %collective-permute-start.39 = (bf16[144,576]{1,0:T(8,128)(2,1)S(1)}, bf16[144,576]{1,0:T(8,128)(2,1)S(1)}, u32[]{:S(2)}, u32[]{:S(2)}) collective-permute-start(bf16[144,576]{1,0:T(8,128)(2,1)S(1)} %dynamic-slice_convert_fusion.1), channel_id=1, source_target_pairs={{0,1},{1,0},{2,3},{3,2},{4,5},{5,4},{6,7},{7,6},{8,9},{9,8},{10,11... | collective-permute-start | bytes 497672 | tf_op jit(solution)/shard_map/ppermute | solution.py:82
  345.4 29.7 %collective-permute-start.21 = (bf16[2,2,144,576]{3,2,1,0:T(8,128)(2,1)S(1)}, bf16[2,2,144,576]{3,2,1,0:T(8,128)(2,1)S(1)}, u32[]{:S(2)}, u32[]{:S(2)}) collective-permute-start(bf16[2,2,144,576]{3,2,1,0:T(8,128)(2,1)S(1)} %dynamic-slice_bitcast_fusion.4), channel_id=1, source_target_pairs={{0,4},{2,6},{4,0},{6,2},{8,12},{10,14},{12,8},{14,10},{16,20},{18,... | collective-permute-start | bytes 1990664 | tf_op jit(solution)/shard_map/ppermute | solution.py:85
  358.4 39.0 %collective-permute-start.27 = (bf16[2,2,216,576]{3,2,1,0:T(8,128)(2,1)S(1)}, bf16[2,2,216,576]{3,2,1,0:T(8,128)(2,1)S(1)}, u32[]{:S(2)}, u32[]{:S(2)}) collective-permute-start(bf16[2,2,216,576]{3,2,1,0:T(8,128)(2,1)S(1)} %dynamic-slice_bitcast_fusion.2), channel_id=1, source_target_pairs={{0,4},{2,6},{4,0},{6,2},{8,12},{10,14},{12,8},{14,10},{16,20},{18,... | collective-permute-start | bytes 2985992 | tf_op jit(solution)/shard_map/ppermute | solution.py:85
  358.7 39.4 %collective-permute-start.43 = (bf16[144,576]{1,0:T(8,128)(2,1)S(1)}, bf16[144,576]{1,0:T(8,128)(2,1)S(1)}, u32[]{:S(2)}, u32[]{:S(2)}) collective-permute-start(bf16[144,576]{1,0:T(8,128)(2,1)S(1)} %dynamic-slice_convert_fusion), channel_id=1, source_target_pairs={{0,1},{1,0},{2,3},{3,2},{4,5},{5,4},{6,7},{7,6},{8,9},{9,8},{10,11... | collective-permute-start | bytes 497672 | tf_op jit(solution)/shard_map/ppermute | solution.py:82
  (84 other events, 916.8 us)
